TPU v7x, 32 devices: a whole 2x2x4 slice. The times are simulated.
32 devices in a mesh: row: 4 (over y, x), col: 8 (over z, core).
Axes of the slice: x: 2, y: 2, z: 4, core: 2. Of those that a mesh axis runs over, the one named last changes fastest.
Arguments:
- pair_state: bfloat16 [1536, 1536, 128], P('row', 'col'), may hold values from -6 to 6
- single_state: bfloat16 [1536, 384], P(('row', 'col')), may hold values from -6 to 6
- token_mask: int32 [1536], P('col'), may hold values 0 or 1
- first_gate: bfloat16 [128, 512], replicated, may hold values from -0.5 to 0.5
- first_up: bfloat16 [128, 512], replicated, may hold values from -0.5 to 0.5
- first_down: bfloat16 [512, 128], replicated, may hold values from -0.25 to 0.25
- bias_weight: bfloat16 [128, 16], replicated, may hold values from -21 to 21
- query_weight: bfloat16 [384, 384], replicated, may hold values from -0.3125 to 0.3125
- key_weight: bfloat16 [384, 384], replicated, may hold values from -0.3125 to 0.3125
- value_weight: bfloat16 [384, 384], replicated, may hold values from -0.3125 to 0.3125
- gate_weight: bfloat16 [384, 384], replicated, may hold values from -0.3125 to 0.3125
- out_weight: bfloat16 [384, 384], replicated, may hold values from -0.3125 to 0.3125
- second_gate: bfloat16 [128, 512], replicated, may hold values from -0.5 to 0.5
- second_up: bfloat16 [128, 512], replicated, may hold values from -0.5 to 0.5
- second_down: bfloat16 [512, 128], replicated, may hold values from -0.25 to 0.25
Outputs:
- pair_out: bfloat16 [1536, 1536, 128], P('row', 'col')
- single_out: bfloat16 [1536, 384], P('row')
All inputs are finite; a program needn't handle non-finite values. No bound on the sum of `token_mask` on one device may be relied on, other than what follows from the above.
Results may differ from a plain program's by a relative error of at most 0.011.
Values may be sent and summed in bfloat16 or wider, within the bound.
A program may use at most 384 MiB of HBM per device.

v0:
```python
import math

import jax
import jax.numpy as jnp
from jax import lax
from jax.sharding import PartitionSpec as P


def spread_2(value, axis, source):
    kept = jnp.where(lax.axis_index(axis) == source, value, 0).astype(value.dtype)
    return lax.psum(kept, axis)


def combined_all(part, axis, combine):
    gathered = jax.tree.map(lambda a: lax.all_gather(a, axis), part)

    def take(source):
        return jax.tree.map(lambda a: lax.dynamic_index_in_dim(a, source, 0, False), gathered)

    return lax.fori_loop(
        1, lax.axis_size(axis), lambda source, state: combine(state, take(source)), take(0)
    )


def norm_rows(values):
    centre = jnp.mean(values, axis=-1, keepdims=True)
    centred = values - centre
    spread = jnp.mean(centred * centred, axis=-1, keepdims=True)
    return centred * lax.rsqrt(spread + 1e-05)


def transition(widened, w_gate, w_up, w_down):
    layout = widened.shape
    flat_cells = widened.reshape(-1, layout[-1])
    normed = norm_rows(flat_cells).astype(jnp.bfloat16)
    gate_act = jnp.dot(normed, w_gate, preferred_element_type=jnp.float32)
    up_act = jnp.dot(normed, w_up, preferred_element_type=jnp.float32)
    hidden = (jax.nn.silu(gate_act) * up_act).astype(jnp.bfloat16)
    return jnp.dot(hidden, w_down, preferred_element_type=jnp.float32).reshape(layout)


def mirror(pair_block):
    row_len, col_len, channels = pair_block.shape
    row_count = lax.axis_size("row")
    shuffled = lax.all_to_all(
        lax.all_to_all(pair_block, "row", split_axis=1, concat_axis=0, tiled=True),
        "col",
        split_axis=0,
        concat_axis=1,
        tiled=True,
    )
    arrived = lax.all_to_all(shuffled, "row", split_axis=1, concat_axis=0, tiled=True)
    arranged = arrived.reshape(row_count, col_len, 2, col_len // row_count, channels)
    return jnp.transpose(arranged, (2, 0, 3, 1, 4)).reshape(row_len, col_len, channels)


def project_keys(key_rows, key_weight, value_weight):
    normed = norm_rows(key_rows.astype(jnp.float32)).astype(jnp.bfloat16)
    key_vecs = jnp.dot(normed, key_weight, preferred_element_type=jnp.float32).astype(jnp.bfloat16)
    value_vecs = jnp.dot(normed, value_weight, preferred_element_type=jnp.float32).astype(
        jnp.bfloat16
    )
    return (key_vecs, value_vecs)


def combine_parts(first, second):
    first_top, first_total, first_sums = first
    second_top, second_total, second_sums = second
    row_top = jnp.maximum(first_top, second_top)
    first_scale = jnp.exp(first_top - row_top)
    second_scale = jnp.exp(second_top - row_top)
    rows_here, head_count = first_top.shape
    merged_sums = (
        first_sums.reshape(rows_here, head_count, -1) * first_scale[:, :, None]
        + second_sums.reshape(rows_here, head_count, -1) * second_scale[:, :, None]
    )
    return (
        row_top,
        first_total * first_scale + second_total * second_scale,
        merged_sums.reshape(first_sums.shape),
    )


def weighted_sums(weights, value_heads, rows_here):
    numerator = jnp.einsum(
        "hij,jhd->ihd", weights, value_heads, precision=lax.Precision.HIGHEST
    ).reshape(rows_here, -1)
    denominator = jnp.transpose(jnp.sum(weights, axis=2), (1, 0))
    return (numerator, denominator)


def body(
    pair_state,
    single_state,
    token_mask,
    first_gate,
    first_up,
    first_down,
    bias_weight,
    query_weight,
    key_weight,
    value_weight,
    gate_weight,
    out_weight,
    second_gate,
    second_up,
    second_down,
):
    rows_here, keys_here, channels = pair_state.shape
    col_index = lax.axis_index("col")
    widened = pair_state.astype(jnp.float32)
    updated = (widened + transition(widened, first_gate, first_up, first_down)).astype(jnp.bfloat16)
    flipped = mirror(updated)
    query_rows = lax.all_gather(single_state, "col", axis=0, tiled=True)
    query_normed = norm_rows(query_rows.astype(jnp.float32)).astype(jnp.bfloat16)
    queries = jnp.dot(query_normed, query_weight, preferred_element_type=jnp.float32).astype(
        jnp.bfloat16
    )
    gate_act = jax.nn.sigmoid(
        jnp.dot(query_normed, gate_weight, preferred_element_type=jnp.float32)
    )
    offset = col_index % 2 * keys_here
    own_rows = lax.dynamic_slice_in_dim(query_rows, offset, keys_here, 0)
    source = col_index // 2
    own_keys, own_values = project_keys(own_rows, key_weight, value_weight)
    both_vecs = spread_2(jnp.stack([own_keys, own_values]), "row", source)
    key_vecs = both_vecs[0]
    value_vecs = both_vecs[1]
    head_count = bias_weight.shape[1]
    head_dim = queries.shape[1] // head_count
    bias_normed = norm_rows(updated.astype(jnp.float32)).astype(jnp.bfloat16)
    pair_bias = jnp.einsum(
        "ijc,ch->hij", bias_normed, bias_weight, preferred_element_type=jnp.float32
    )
    scores = (
        jnp.einsum(
            "ihd,jhd->hij",
            queries.reshape(rows_here, head_count, head_dim),
            key_vecs.reshape(keys_here, head_count, head_dim),
            preferred_element_type=jnp.float32,
        )
        * (1.0 / math.sqrt(head_dim))
        + pair_bias
    )
    scores = jnp.where(token_mask[None, None, :] > 0, scores, -1000000000.0)
    value_heads = value_vecs.astype(jnp.float32).reshape(keys_here, head_count, head_dim)
    local_top = jnp.transpose(jnp.max(scores, axis=2), (1, 0))
    weights = jnp.exp(scores - jnp.transpose(local_top, (1, 0))[:, :, None])
    numerator, denominator = weighted_sums(weights, value_heads, rows_here)
    row_top, denominator, numerator = combined_all(
        (local_top, denominator, numerator), "col", combine_parts
    )
    attended = (
        numerator.reshape(rows_here, head_count, head_dim) / denominator[:, :, None]
    ).reshape(rows_here, -1)
    gated = (gate_act * attended).astype(jnp.bfloat16)
    single_out = (
        query_rows.astype(jnp.float32)
        + jnp.dot(gated, out_weight, preferred_element_type=jnp.float32)
    ).astype(jnp.bfloat16)
    summed = updated.astype(jnp.float32) + flipped.astype(jnp.float32)
    pair_out = (summed + transition(summed, second_gate, second_up, second_down)).astype(
        jnp.bfloat16
    )
    return (pair_out, single_out)


def solution(mesh):
    in_specs = (
        P("row", "col", None),
        P(("row", "col"), None),
        P("col"),
        P(),
        P(),
        P(),
        P(),
        P(),
        P(),
        P(),
        P(),
        P(),
        P(),
        P(),
        P(),
    )
    out_specs = (P("row", "col", None), P("row", None))
    return jax.shard_map(body, mesh=mesh, in_specs=in_specs, out_specs=out_specs, check_vma=False)
```

profile of v0, /device:TPU:13, one launch (start us, length us, event | category | flops | bytes accessed | tf_op | source)
XLA Modules:
  0.0 1650.1 jit_solution(15566759404232184608)
XLA Ops:
  7.2 12.6 convert_reduce_fusion.1
  20.0 26.9 %multiply_reduce_fusion.1 = f32[384,192]{1,0:T(8,128)S(1)} fusion(bf16[384,192,128]{2,1,0:T(8,128)(2,1)} %param.17, f32[384,192]{1,0:T(8,128)S(1)} %broadcast_multiply_fusion.2), kind=kLoop, calls=%fused_computation.31 | loop fusion | flops 37675008 | bytes 19464192 | tf_op jit(solution)/shard_map/reduce_sum | solution.py:28
  47.2 42.1 %fusion.11 = bf16[73728,128]{1,0:T(8,128)(2,1)} fusion(bf16[384,192,128]{2,1,0:T(8,128)(2,1)} %param.17, f32[73728]{0:T(1024)S(1)} %rsqrt.47, f32[73728]{0:T(1024)S(1)} %div.64), kind=kLoop, calls=%fused_computation.27 | loop fusion | flops 37748736 | bytes 38338560 | tf_op jit(solution)/shard_map/convert_element_type | solution.py:35
  89.3 56.8 %fusion.59 = f32[73728,512]{1,0:T(8,128)} fusion(bf16[73728,128]{1,0:T(8,128)(2,1)} %fusion.11, bf16[128,512]{1,0:T(8,128)(2,1)S(1)} %copy-done.9), kind=kOutput, calls=%fused_computation.95 | convolution fusion | flops 9663676416 | bytes 170000384 | tf_op jit(solution)/shard_map/dot_general | solution.py:36
  146.1 75.6 %fusion.12 = f32[73728,128]{1,0:T(8,128)} fusion(bf16[512,128]{1,0:T(8,128)(2,1)S(1)} %copy-done.18, f32[73728,512]{1,0:T(8,128)} %fusion.59, bf16[73728,128]{1,0:T(8,128)(2,1)} %fusion.11, bf16[128,512]{1,0:T(8,128)(2,1)S(1)} %copy-done.19), kind=kOutput, calls=%fused_computation.33 | convolution fusion | flops 19553845248 | bytes 207880192 | tf_op jit(solution)/shard_map/dot_general | solution.py:39
  221.7 26.1 %convert_reduce_fusion = (f32[384,192]{1,0:T(8,128)S(1)}, bf16[384,192,128]{2,1,0:T(8,128)(2,1)}) fusion(f32[384,192,128]{2,1,0:T(8,128)} %bitcast.123, bf16[384,192,128]{2,1,0:T(8,128)(2,1)} %param.17), kind=kLoop, calls=%fused_computation.16 | loop fusion | flops 47112192 | bytes 75792384 | tf_op jit(solution)/shard_map/reduce_sum | solution.py:26
  247.8 16.4 copy.60
  264.2 206.9 %all_to_all.48 = bf16[384,192,128]{2,0,1:T(8,128)(2,1)S(1)} all-to-all(bf16[384,192,128]{2,0,1:T(8,128)(2,1)S(1)} %copy.60), channel_id=1, replica_groups=mesh['row'=4,'col'=8] {'row'}, dimensions={1} | all-to-all | bytes 37748736 | tf_op jit(solution)/shard_map/all_to_all | solution.py:46
  471.1 52.0 %copy.62 = bf16[4,384,48,128]{3,2,1,0:T(8,128)(2,1)S(1)} copy(bf16[4,384,48,128]{3,1,2,0:T(8,128)(2,1)S(1)} %bitcast.119) | data formatting | bytes 37748736 | tf_op jit(solution)/shard_map/all_to_all | solution.py:46
  523.1 413.0 %all_to_all.49 = bf16[1536,48,128]{2,1,0:T(8,128)(2,1)S(1)} all-to-all(bf16[1536,48,128]{2,1,0:T(8,128)(2,1)S(1)} %bitcast.120), channel_id=1, replica_groups=mesh['row'=4,'col'=8] {'col'}, dimensions={0} | all-to-all | bytes 37748736 | tf_op jit(solution)/shard_map/all_to_all | solution.py:45
  938.7 43.5 %copy.64 = bf16[192,384,128]{2,0,1:T(8,128)(2,1)} copy(bf16[192,384,128]{2,1,0:T(8,128)(2,1)S(1)} %bitcast.122) | data formatting | bytes 37748736 | tf_op jit(solution)/shard_map/all_to_all | solution.py:45
  990.3 14.4 all_gather.18
  1007.7 213.5 %all-reduce.2.cloned.1.call-done = bf16[2,192,384]{2,1,0:T(8,128)(2,1)} async-done(((bf16[2,192,384]{2,1,0:T(8,128)(2,1)}), bf16[2,192,384]{2,1,0:T(8,128)(2,1)}) %all-reduce.2.cloned.1.call-update) | async-done | bytes 294928 | tf_op jit(solution)/shard_map/psum | solution.py:11
  1222.5 20.8 %copy.65 = bf16[192,384,128]{2,1,0:T(8,128)(2,1)} copy(bf16[192,384,128]{2,0,1:T(8,128)(2,1)} %all-to-all-done.2) | data formatting | bytes 37748736 | tf_op jit(solution)/shard_map/all_to_all | solution.py:52
  1254.7 24.0 %copy.67 = f32[2,4,48,192,128]{4,3,2,1,0:T(8,128)} copy(f32[2,4,48,192,128]{4,2,0,1,3:T(8,128)S(1)} %bitcast.117) | data formatting | bytes 75497472 | tf_op jit(solution)/shard_map/convert_element_type | solution.py:161
  1278.7 41.6 %fusion.56 = (f32[384,192]{1,0:T(8,128)S(1)}, f32[384,192,128]{2,1,0:T(8,128)}, f32[384,192]{1,0:T(8,128)S(1)}) fusion(f32[384,192,128]{2,1,0:T(8,128)} %bitcast.116, bf16[384,192,128]{2,1,0:T(8,128)(2,1)} %get-tuple-element.228, f32[384,192]{1,0:T(8,128)S(1)} %broadcast_multiply_fusion), kind=kLoop, calls=%fused_computation.92 | loop fusion | flops 56475648 | bytes 95256576 | tf_op jit(solution)/shard_map/reduce_sum | solution.py:26
  1320.4 25.9 %fusion.14 = f32[384,192,16]{1,2,0:T(8,128)} fusion(bf16[384,192,128]{2,1,0:T(8,128)(2,1)} %get-tuple-element.228, f32[384,192]{1,0:T(8,128)S(1)} %get-tuple-element.238, f32[384,192]{1,0:T(8,128)S(1)} %broadcast_multiply_fusion, bf16[128,16]{0,1:T(8,128)(2,1)S(1)} %copy-done.22), kind=kOutput, calls=%fused_computation.35 | convolution fusion | flops 339738624 | bytes 24186880 | tf_op jit(solution)/shard_map/ijc,ch->hij/dot_general | solution.py:132
  1362.1 26.3 %multiply_reduce_fusion = f32[384,192]{1,0:T(8,128)S(1)} fusion(f32[384,192,128]{2,1,0:T(8,128)} %get-tuple-element.230, f32[384,192]{1,0:T(8,128)S(1)} %get-tuple-element.239), kind=kLoop, calls=%fused_computation.29 | loop fusion | flops 28237824 | bytes 38338560 | tf_op jit(solution)/shard_map/reduce_sum | solution.py:28
  1388.7 42.6 %fusion.9 = bf16[73728,128]{1,0:T(8,128)(2,1)} fusion(f32[384,192,128]{2,1,0:T(8,128)} %get-tuple-element.230, f32[73728]{0:T(1024)S(1)} %rsqrt.49, f32[73728]{0:T(1024)S(1)} %div.68), kind=kLoop, calls=%fused_computation.24 | loop fusion | flops 28311552 | bytes 57212928 | tf_op jit(solution)/shard_map/convert_element_type | solution.py:35
  1431.3 56.8 %fusion.60 = f32[73728,512]{1,0:T(8,128)} fusion(bf16[73728,128]{1,0:T(8,128)(2,1)} %fusion.9, bf16[128,512]{1,0:T(8,128)(2,1)S(1)} %copy-done.10), kind=kOutput, calls=%fused_computation.96 | convolution fusion | flops 9663676416 | bytes 170000384 | tf_op jit(solution)/shard_map/dot_general | solution.py:36
  1488.1 75.8 %fusion.13 = f32[73728,128]{1,0:T(8,128)} fusion(bf16[512,128]{1,0:T(8,128)(2,1)S(1)} %copy-done.20, f32[73728,512]{1,0:T(8,128)} %fusion.60, bf16[73728,128]{1,0:T(8,128)(2,1)} %fusion.9, bf16[128,512]{1,0:T(8,128)(2,1)S(1)} %copy-done.21), kind=kOutput, calls=%fused_computation.34 | convolution fusion | flops 19553845248 | bytes 207880192 | tf_op jit(solution)/shard_map/dot_general | solution.py:39
  1566.9 15.0 all-gather.1
  1581.9 14.1 all-gather
  1596.2 31.3 %add_convert_fusion = bf16[384,192,128]{2,1,0:T(8,128)(2,1)} fusion(f32[384,192,128]{2,1,0:T(8,128)} %get-tuple-element.230, f32[384,192,128]{2,1,0:T(8,128)} %bitcast.124), kind=kLoop, calls=%fused_computation.28 | loop fusion | flops 18874368 | bytes 94371840 | tf_op jit(solution)/shard_map/convert_element_type | solution.py:162
  (133 shorter events, 72.8 us)
Async XLA Ops:
  7.2 1000.0 %copy-start = (bf16[384,384]{1,0:T(8,128)(2,1)S(1)}, bf16[384,384]{1,0:T(8,128)(2,1)}, u32[]{:S(2)}) copy-start(bf16[384,384]{1,0:T(8,128)(2,1)} %param.24) | copy-start | bytes 884740
  7.2 82.1 %copy-start.9 = (bf16[128,512]{1,0:T(8,128)(2,1)S(1)}, bf16[128,512]{1,0:T(8,128)(2,1)}, u32[]{:S(2)}) copy-start(bf16[128,512]{1,0:T(8,128)(2,1)} %param.20) | copy-start | bytes 393220
  89.3 56.8 %copy-start.18 = (bf16[512,128]{1,0:T(8,128)(2,1)S(1)}, bf16[512,128]{1,0:T(8,128)(2,1)}, u32[]{:S(2)}) copy-start(bf16[512,128]{1,0:T(8,128)(2,1)} %param.22) | copy-start | bytes 393220
  89.3 56.8 %copy-start.19 = (bf16[128,512]{1,0:T(8,128)(2,1)S(1)}, bf16[128,512]{1,0:T(8,128)(2,1)}, u32[]{:S(2)}) copy-start(bf16[128,512]{1,0:T(8,128)(2,1)} %param.21) | copy-start | bytes 393220
  938.7 51.6 %copy-start.11 = (bf16[48,384]{1,0:T(8,128)(2,1)S(1)}, bf16[48,384]{1,0:T(8,128)(2,1)}, u32[]{:S(2)}) copy-start(bf16[48,384]{1,0:T(8,128)(2,1)} %param.18) | copy-start | bytes 110596
  938.7 66.4 %copy-start.7 = (bf16[384,384]{1,0:T(8,128)(2,1)S(1)}, bf16[384,384]{1,0:T(8,128)(2,1)}, u32[]{:S(2)}) copy-start(bf16[384,384]{1,0:T(8,128)(2,1)} %param.26) | copy-start | bytes 884740
  938.7 66.7 %copy-start.8 = (bf16[384,384]{1,0:T(8,128)(2,1)S(1)}, bf16[384,384]{1,0:T(8,128)(2,1)}, u32[]{:S(2)}) copy-start(bf16[384,384]{1,0:T(8,128)(2,1)} %param.25) | copy-start | bytes 884740
  938.7 68.5 %copy-start.23 = (s32[192]{0:T(256)S(1)}, s32[192]{0:T(256)}, u32[]{:S(2)}) copy-start(s32[192]{0:T(256)} %param.19) | copy-start | bytes 2308
  982.2 240.4 %all-to-all-start.2 = ((bf16[192,384,128]{2,0,1:T(8,128)(2,1)}), bf16[192,384,128]{2,0,1:T(8,128)(2,1)}, u32[]{:S(2)}, u32[]{:S(2)}) async-start(bf16[192,384,128]{2,0,1:T(8,128)(2,1)} %copy.64), calls=%async_computation.2 | async-start | bytes 37748736 | tf_op jit(solution)/shard_map/all_to_all | solution.py:52
  990.3 230.9 %all-reduce.2.cloned.1.call-start = ((), (), s32[]{:S(2)}) async-start(), calls=%async_computation.3 | async-start | bytes 589824 | tf_op jit(solution)/shard_map/psum | solution.py:11
  1004.7 238.6 %copy-start.3 = (bf16[384,384]{1,0:T(8,128)(2,1)}, bf16[384,384]{1,0:T(8,128)(2,1)S(1)}, u32[]{:S(2)}) copy-start(bf16[384,384]{1,0:T(8,128)(2,1)S(1)} %all_gather.18) | copy-start | bytes 884740
  1006.5 621.0 %all-gather.4.cloned.1.call-start = ((), (), s32[]{:S(2)}) async-start(), calls=%async_computation.4 | async-start | bytes 5308416 | tf_op jit(solution)/shard_map/all_gather | solution.py:15
  1006.9 215.5 %copy-start.12 = (f32[384]{0:T(512)}, f32[384]{0:T(512)S(1)}, u32[]{:S(2)}) copy-start(f32[384]{0:T(512)S(1)} %broadcast_multiply_fusion.3) | copy-start | bytes 4612
  1007.1 215.2 %copy-start.14 = (f32[384]{0:T(512)}, f32[384]{0:T(512)S(1)}, u32[]{:S(2)}) copy-start(f32[384]{0:T(512)S(1)} %add_rsqrt_fusion.3) | copy-start | bytes 4612
  1388.4 42.9 %copy-start.10 = (bf16[128,512]{1,0:T(8,128)(2,1)S(1)}, bf16[128,512]{1,0:T(8,128)(2,1)}, u32[]{:S(2)}) copy-start(bf16[128,512]{1,0:T(8,128)(2,1)} %param.29) | copy-start | bytes 393220
  1431.3 56.8 %copy-start.20 = (bf16[512,128]{1,0:T(8,128)(2,1)S(1)}, bf16[512,128]{1,0:T(8,128)(2,1)}, u32[]{:S(2)}) copy-start(bf16[512,128]{1,0:T(8,128)(2,1)} %param.31) | copy-start | bytes 393220
  1431.3 56.8 %copy-start.21 = (bf16[128,512]{1,0:T(8,128)(2,1)S(1)}, bf16[128,512]{1,0:T(8,128)(2,1)}, u32[]{:S(2)}) copy-start(bf16[128,512]{1,0:T(8,128)(2,1)} %param.30) | copy-start | bytes 393220
  1488.1 75.8 %copy-start.6 = (f32[16,384]{1,0:T(8,128)S(1)}, f32[16,384]{1,0:T(8,128)}, u32[]{:S(2)}) copy-start(f32[16,384]{1,0:T(8,128)} %copy-done.5) | copy-start | bytes 73732
  1596.1 45.1 %copy-start.4 = (bf16[384,384]{1,0:T(8,128)(2,1)S(1)}, bf16[384,384]{1,0:T(8,128)(2,1)}, u32[]{:S(2)}) copy-start(bf16[384,384]{1,0:T(8,128)(2,1)} %copy-done.3) | copy-start | bytes 884740
  1596.1 45.1 %copy-start.13 = (f32[384]{0:T(512)S(1)}, f32[384]{0:T(512)}, u32[]{:S(2)}) copy-start(f32[384]{0:T(512)} %copy-done.12) | copy-start | bytes 4612
  1596.1 45.1 %copy-start.15 = (f32[384]{0:T(512)S(1)}, f32[384]{0:T(512)}, u32[]{:S(2)}) copy-start(f32[384]{0:T(512)} %copy-done.14) | copy-start | bytes 4612
  1596.2 45.1 %copy-start.16 = (bf16[384,384]{1,0:T(8,128)(2,1)S(1)}, bf16[384,384]{1,0:T(8,128)(2,1)}, u32[]{:S(2)}) copy-start(bf16[384,384]{1,0:T(8,128)(2,1)} %param.28) | copy-start | bytes 884740
  1596.2 45.1 %copy-start.17 = (bf16[384,384]{1,0:T(8,128)(2,1)S(1)}, bf16[384,384]{1,0:T(8,128)(2,1)}, u32[]{:S(2)}) copy-start(bf16[384,384]{1,0:T(8,128)(2,1)} %param.27) | copy-start | bytes 884740
  1596.2 46.6 %copy-start.1 = (bf16[384,384]{1,0:T(8,128)(2,1)S(1)}, bf16[384,384]{1,0:T(8,128)(2,1)}, u32[]{:S(2)}) copy-start(bf16[384,384]{1,0:T(8,128)(2,1)} %param.24) | copy-start | bytes 884740
  (3 other events, 49.3 us)
Sparse Core Ops, SparseCore 0:
  1006.6 214.5 all-reduce.1
  1362.0 51.1 all-gather.3
where the time goes:
time: 1660 us; the launch traced here: 1650 us
  blocking collectives  663 us (40%)
  matrix products  300 us (18%)
  other arithmetic  267 us (16%)
  waiting for transfers between devices  214 us (13%)
  local copies, waits for them, and re-layouts  183 us (11%)
    all_to_all x1, blocking collectives, mirror(): lax.all_to_all(lax.all_to_all(pair_block, 'row', split_axis=1, concat_axi...  413 us
    psum x1, waiting for transfers between devices, spread_2(): return lax.psum(kept, axis)  214 us
    all_to_all x1, blocking collectives, mirror(): lax.all_to_all(pair_block, 'row', split_axis=1, concat_axis=0, tiled=True)  207 us
    dot_general x2, matrix products, transition(): jnp.dot(hidden, w_down, preferred_element_type=jnp.float32).reshape(layout)  151 us
    dot_general x2, matrix products, transition(): gate_act = jnp.dot(normed, w_gate, preferred_element_type=jnp.float32)  114 us
    convert_element_type x2, other arithmetic, transition(): normed = norm_rows(flat_cells).astype(jnp.bfloat16)  84.6 us
    reduce_sum x5, other arithmetic, norm_rows(): centre = jnp.mean(values, axis=-1, keepdims=True)  80.5 us
    reduce_sum x4, other arithmetic, norm_rows(): spread = jnp.mean(centred * centred, axis=-1, keepdims=True)  53.6 us
  transfers between devices with their start and end apart: 3, of which 1 were waited for; matrix products, arithmetic and copies ran while one was open for 15% of the time, Pallas kernels for 0%

commit v1 on v0

v1 whole, which is shorter than its diff:
```python
import functools
import math

import jax
import jax.numpy as jnp
from jax import lax
from jax.experimental import pallas as pl
from jax.experimental.pallas import tpu as pltpu
from jax.sharding import PartitionSpec as P

VMEM_LIMIT = 56 * 1024 * 1024


def norm_rows(values):
    centre = jnp.mean(values, axis=-1, keepdims=True)
    centred = values - centre
    spread = jnp.mean(centred * centred, axis=-1, keepdims=True)
    return centred * lax.rsqrt(spread + 1e-05)


def transition(cells, w_in, w_down):
    normed = norm_rows(cells).astype(jnp.bfloat16)
    both = jnp.dot(normed, w_in, preferred_element_type=jnp.float32)
    hid = both.shape[1] // 2
    half_gate = both[:, :hid]
    hidden = (half_gate * (1.0 + jnp.tanh(half_gate)) * both[:, hid:]).astype(jnp.bfloat16)
    return cells + jnp.dot(hidden, w_down, preferred_element_type=jnp.float32)


def first_kernel(pair_ref, w_in_ref, w_down_ref, bias_w_ref, updated_ref, bias_ref):
    rows, cols, channels = pair_ref.shape
    cells = pair_ref[...].reshape(rows * cols, channels).astype(jnp.float32)
    updated = transition(cells, w_in_ref[...], w_down_ref[...]).astype(jnp.bfloat16)
    updated_ref[...] = updated.reshape(rows, cols, channels)
    normed = norm_rows(updated.astype(jnp.float32)).astype(jnp.bfloat16)
    bias_ref[...] = lax.dot_general(
        bias_w_ref[...], normed, (((1,), (1,)), ((), ())), preferred_element_type=jnp.float32
    )


def first_pass(pair_state, w_in, w_down, bias_t):
    rows, cols, channels = pair_state.shape
    heads = bias_t.shape[0]
    step = math.gcd(rows, 8)
    whole = lambda a: pl.BlockSpec(a.shape, lambda i: (0, 0))
    return pl.pallas_call(
        first_kernel,
        grid=(rows // step,),
        in_specs=[
            pl.BlockSpec((step, cols, channels), lambda i: (i, 0, 0)),
            whole(w_in),
            whole(w_down),
            whole(bias_t),
        ],
        out_specs=[
            pl.BlockSpec((step, cols, channels), lambda i: (i, 0, 0)),
            pl.BlockSpec((heads, step * cols), lambda i: (0, i)),
        ],
        out_shape=[
            jax.ShapeDtypeStruct(pair_state.shape, jnp.bfloat16),
            jax.ShapeDtypeStruct((heads, rows * cols), jnp.float32),
        ],
        compiler_params=pltpu.CompilerParams(vmem_limit_bytes=VMEM_LIMIT),
    )(pair_state, w_in, w_down, bias_t)


def second_kernel(updated_ref, arrived_ref, w_in_ref, w_down_ref, out_ref):
    rows, cols, channels = updated_ref.shape
    flipped = jnp.swapaxes(arrived_ref[0].astype(jnp.float32), 0, 1)
    summed = updated_ref[...].astype(jnp.float32) + flipped
    part = rows // 2
    for start in range(0, rows, part):
        cells = summed[start : start + part].reshape(part * cols, channels)
        made = transition(cells, w_in_ref[...], w_down_ref[...]).astype(jnp.bfloat16)
        out_ref[start : start + part] = made.reshape(part, cols, channels)


def second_pass(updated, arrived, w_in, w_down):
    rows, cols, channels = updated.shape
    sources = arrived.shape[0]
    span = rows // sources
    step = math.gcd(span, 16)
    blocks = span // step
    whole = lambda a: pl.BlockSpec(a.shape, lambda s, i: (0, 0))
    own = pl.BlockSpec((step, cols, channels), lambda s, i: (s * blocks + i, 0, 0))
    return pl.pallas_call(
        second_kernel,
        grid=(sources, blocks),
        in_specs=[
            own,
            pl.BlockSpec((1, cols, step, channels), lambda s, i: (s, 0, i, 0)),
            whole(w_in),
            whole(w_down),
        ],
        out_specs=own,
        out_shape=jax.ShapeDtypeStruct(updated.shape, jnp.bfloat16),
        compiler_params=pltpu.CompilerParams(vmem_limit_bytes=VMEM_LIMIT),
    )(updated, arrived, w_in, w_down)


MESH = pl.DeviceIdType.MESH


class Exchange:
    def __init__(self, row_count, col_count, chunks, own, first, second, last, sems):
        self.row_count, self.col_count = row_count, col_count
        self.rep = col_count // row_count
        self.own, self.first, self.second, self.last = own, first, second, last
        self.sems = sems
        self.size = own.shape[2] // chunks
        self.row, self.col = lax.axis_index("row"), lax.axis_index("col")

    def rows(self, chunk):
        return pl.ds(chunk * self.size, self.size)

    def hop(self, number, chunk, offset, local=False):
        rows = self.rows(chunk)
        row, col, rep = self.row, self.col, self.rep
        if number == 1:
            to = lax.rem(row + offset, self.row_count)
            source, target = self.own.at[:, to, rows], self.first.at[row, :, rows]
            device = (to, col)
        elif number == 2:
            to = lax.rem(col + offset, self.col_count)
            source = self.first.at[to // rep, lax.rem(to, rep), rows]
            target = self.second.at[col, rows]
            device = (row, to)
        else:
            to = lax.rem(row + offset, self.row_count)
            source = self.second.at[pl.ds(to * rep, rep), rows]
            target = self.last.at[:, row, rows]
            device = (to, col)
        send, recv = self.sems[2 * number - 2], self.sems[2 * number - 1]
        if local:
            return pltpu.make_async_copy(source, target, recv.at[chunk, 0])
        return pltpu.make_async_remote_copy(
            src_ref=source,
            dst_ref=target,
            send_sem=send.at[chunk, offset],
            recv_sem=recv.at[chunk, offset],
            device_id=device,
            device_id_type=MESH,
        )

    def count(self, number):
        return self.col_count if number == 2 else self.row_count

    def each(self, number, act):
        def step(offset, carry):
            act(offset)
            return carry

        lax.fori_loop(1, self.count(number), step, 0)

    def start(self, number, chunk):
        self.each(number, lambda o: self.hop(number, chunk, o).start())
        self.hop(number, chunk, 0, True).start()

    def arrive(self, number, chunk):
        self.each(number, lambda o: self.hop(number, chunk, o).wait_recv())
        self.hop(number, chunk, 0, True).wait()

    def finish(self, number, chunk):
        self.each(number, lambda o: self.hop(number, chunk, o).wait_send())

    def greet(self):
        barrier = pltpu.get_barrier_semaphore()

        def in_col(offset):
            to = lax.rem(self.row + offset, self.row_count)
            pl.semaphore_signal(barrier, inc=1, device_id=(to, self.col), device_id_type=MESH)

        def in_row(offset):
            to = lax.rem(self.col + offset, self.col_count)
            pl.semaphore_signal(barrier, inc=1, device_id=(self.row, to), device_id_type=MESH)

        self.each(1, in_col)
        self.each(2, in_row)
        pl.semaphore_wait(barrier, self.row_count + self.col_count - 2)


def exchange_kernel(row_count, col_count, chunks, own, first, second, last, *sems):
    trip = Exchange(row_count, col_count, chunks, own, first, second, last, sems)
    trip.greet()
    for step in range(chunks + 2):
        if step < chunks:
            trip.start(1, step)
        if 1 <= step <= chunks:
            trip.arrive(1, step - 1)
            trip.start(2, step - 1)
        if step >= 2:
            trip.arrive(2, step - 2)
            trip.start(3, step - 2)
    for chunk in range(chunks):
        trip.arrive(3, chunk)
        for number in (1, 2, 3):
            trip.finish(number, chunk)


def mirror(updated):
    rows, cols, channels = updated.shape
    row_count, col_count = lax.axis_size("row"), lax.axis_size("col")
    rep = col_count // row_count
    part = rows // rep // row_count
    chunks = math.gcd(part, 6)
    sems = []
    for count in (row_count, col_count, row_count):
        sems += [pltpu.SemaphoreType.DMA((chunks, count))] * 2
    shape = lambda *lead: jax.ShapeDtypeStruct((*lead, part, cols, channels), jnp.bfloat16)
    outs = pl.pallas_call(
        functools.partial(exchange_kernel, row_count, col_count, chunks),
        in_specs=[pl.BlockSpec(memory_space=pl.ANY)],
        out_specs=[pl.BlockSpec(memory_space=pl.ANY)] * 3,
        out_shape=[shape(row_count, rep), shape(col_count), shape(rep, row_count)],
        scratch_shapes=sems,
        compiler_params=pltpu.CompilerParams(
            collective_id=0, has_side_effects=True, vmem_limit_bytes=VMEM_LIMIT
        ),
    )(updated.reshape(rep, row_count, part, cols, channels))
    return outs[2].reshape(rep, cols, cols, channels)


def spread_2(value, axis, source):
    kept = jnp.where(lax.axis_index(axis) == source, value, 0).astype(value.dtype)
    return lax.psum(kept, axis)


def project_keys(key_rows, key_weight, value_weight):
    normed = norm_rows(key_rows.astype(jnp.float32)).astype(jnp.bfloat16)
    key_vecs = jnp.dot(normed, key_weight, preferred_element_type=jnp.float32).astype(jnp.bfloat16)
    value_vecs = jnp.dot(normed, value_weight, preferred_element_type=jnp.float32).astype(
        jnp.bfloat16
    )
    return (key_vecs, value_vecs)


def combined(numerator, total, top, axis):
    width, heads = numerator.shape[1], top.shape[1]
    parts = lax.all_gather(jnp.concatenate([numerator, total, top], axis=1), axis)
    tops = parts[:, :, width + heads :]
    scale = jnp.exp(tops - jnp.max(tops, axis=0))
    wide = jnp.repeat(scale, width // heads, axis=2)
    return (
        jnp.sum(parts[:, :, :width] * wide, axis=0),
        jnp.sum(parts[:, :, width : width + heads] * scale, axis=0),
    )


def body(
    pair_state,
    single_state,
    token_mask,
    first_gate,
    first_up,
    first_down,
    bias_weight,
    query_weight,
    key_weight,
    value_weight,
    gate_weight,
    out_weight,
    second_gate,
    second_up,
    second_down,
):
    rows_here, keys_here, channels = pair_state.shape
    col_index = lax.axis_index("col")
    first_in = jnp.concatenate([first_gate * 0.5, first_up], axis=1)
    second_in = jnp.concatenate([second_gate * 0.5, second_up], axis=1)
    updated, flat_bias = first_pass(pair_state, first_in, first_down, bias_weight.T)
    arrived = mirror(updated)
    query_rows = lax.all_gather(single_state, "col", axis=0, tiled=True)
    query_normed = norm_rows(query_rows.astype(jnp.float32)).astype(jnp.bfloat16)
    queries = jnp.dot(query_normed, query_weight, preferred_element_type=jnp.float32).astype(
        jnp.bfloat16
    )
    gate_act = jax.nn.sigmoid(
        jnp.dot(query_normed, gate_weight, preferred_element_type=jnp.float32)
    )
    rep = rows_here // keys_here
    own_rows = lax.dynamic_slice_in_dim(query_rows, col_index % rep * keys_here, keys_here, 0)
    own_keys, own_values = project_keys(own_rows, key_weight, value_weight)
    both_vecs = spread_2(jnp.stack([own_keys, own_values]), "row", col_index // rep)
    key_vecs, value_vecs = both_vecs[0], both_vecs[1]
    head_count = bias_weight.shape[1]
    head_dim = queries.shape[1] // head_count
    pair_bias = flat_bias.reshape(head_count, rows_here, keys_here)
    scores = (
        jnp.einsum(
            "ihd,jhd->hij",
            queries.reshape(rows_here, head_count, head_dim),
            key_vecs.reshape(keys_here, head_count, head_dim),
            preferred_element_type=jnp.float32,
        )
        * (1.0 / math.sqrt(head_dim))
        + pair_bias
    )
    scores = jnp.where(token_mask[None, None, :] > 0, scores, -1000000000.0)
    value_heads = value_vecs.astype(jnp.float32).reshape(keys_here, head_count, head_dim)
    local_top = jnp.max(scores, axis=2)
    weights = jnp.exp(scores - local_top[:, :, None])
    numerator = jnp.einsum(
        "hij,jhd->ihd", weights, value_heads, precision=lax.Precision.HIGHEST
    ).reshape(rows_here, -1)
    numerator, total = combined(numerator, jnp.sum(weights, axis=2).T, local_top.T, "col")
    attended = (
        numerator.reshape(rows_here, head_count, head_dim) / total[:, :, None]
    ).reshape(rows_here, -1)
    gated = (gate_act * attended).astype(jnp.bfloat16)
    single_out = (
        query_rows.astype(jnp.float32)
        + jnp.dot(gated, out_weight, preferred_element_type=jnp.float32)
    ).astype(jnp.bfloat16)
    pair_out = second_pass(updated, arrived, second_in, second_down)
    return (pair_out, single_out)


def solution(mesh):
    in_specs = (P("row", "col", None), P(("row", "col"), None), P("col")) + (P(),) * 12
    out_specs = (P("row", "col", None), P("row", None))
    return jax.shard_map(body, mesh=mesh, in_specs=in_specs, out_specs=out_specs, check_vma=False)
```

time: 1660 us -> 754 us (0.45)
  Pallas kernels: 0 us -> 687 us
  blocking collectives: 663 us -> 15.2 us
  matrix products: 300 us -> 10.7 us
  other arithmetic: 267 us -> 8.93 us
  waiting for transfers between devices: 214 us -> 0.06 us
  local copies, waits for them, and re-layouts: 183 us -> 17.2 us
    pallas_call x0 -> x3, Pallas kernels: none -> 687 us  [the longest x1 488 us: mirror(): pl.pallas_call(functools.partial(exchange_kernel, row_count, col_count, c...]
    all_to_all x2 -> x0, blocking collectives: 620 us -> none  [the longest x1 413 us: mirror(): lax.all_to_all(lax.all_to_all(pair_block, 'row', split_axis=1, concat_axi...]
    dot_general x6 -> x1, matrix products: 293 us -> 2.3 us  [body(): jnp.einsum('hij,jhd->ihd', weights, value_heads, precision=lax.Precision....]
    psum x1, waiting for transfers between devices: 214 us -> 0.02 us  [spread_2(): return lax.psum(kept, axis)]
    convert_element_type x4 -> x0, other arithmetic: 127 us -> none  [the longest x2 84.6 us: transition(): normed = norm_rows(flat_cells).astype(jnp.bfloat16)]
    all_to_all x4 -> x0, local copies, waits for them, and re-layouts: 119 us -> none  [the longest x1 52 us: mirror(): lax.all_to_all(pair_block, 'row', split_axis=1, concat_axis=0, tiled=True)]
    reduce_sum x5 -> x2, other arithmetic: 80.5 us -> 0.26 us  [norm_rows(): centre = jnp.mean(values, axis=-1, keepdims=True)]
    reduce_sum x4 -> x2, other arithmetic: 53.6 us -> 0.46 us  [norm_rows(): spread = jnp.mean(centred * centred, axis=-1, keepdims=True)]
  transfers between devices with their start and end apart: 3 -> 2, of which waited for: 1 -> 0; matrix products, arithmetic and copies ran while one was open for 15% -> 2% of each run, Pallas kernels for 0% -> 91%
where the time goes in v1:
time: 754 us
  Pallas kernels  687 us (91%)
  local copies, waits for them, and re-layouts  17.2 us (2%)
  blocking collectives  15.2 us (2%)
  between operations  14.3 us (2%)
  matrix products  10.7 us (1%)
  other arithmetic  8.93 us (1%)
    pallas_call x1, Pallas kernels, mirror(): pl.pallas_call(functools.partial(exchange_kernel, row_count, col_count, c...  488 us
    pallas_call x1, Pallas kernels, first_pass(): pl.pallas_call(first_kernel, grid=(rows // step,), in_specs=[pl.BlockSpec...  113 us
    pallas_call x1, Pallas kernels, second_pass(): pl.pallas_call(second_kernel, grid=(sources, blocks), in_specs=[own, pl.B...  86.2 us
    all_gather x1, blocking collectives, body(): query_rows = lax.all_gather(single_state, 'col', axis=0, tiled=True)  15.2 us
  transfers between devices with their start and end apart: 2, of which 0 were waited for; matrix products, arithmetic and copies ran while one was open for 2% of the time, Pallas kernels for 91%

profile of v1, /device:TPU:13, one launch (start us, length us, event | category | flops | bytes accessed | tf_op | source)
XLA Modules:
  0.0 753.9 jit_solution(5860080326044269538)
XLA Ops:
  7.2 15.2 %all_gather.9 = bf16[384,384]{1,0:T(8,128)(2,1)S(1)} all-gather(bf16[48,384]{1,0:T(8,128)(2,1)} %param.16), channel_id=1, replica_groups=mesh['row'=4,'col'=8] {'col'}, dimensions={0}, use_global_device_ids=true | all-gather | bytes 331776 | tf_op jit(solution)/shard_map/all_gather | solution.py:272
  22.6 0.2 fusion.21
  22.8 1.3 fusion.10
  24.1 1.3 fusion.11
  25.4 0.8 maximum_select_fusion
  26.4 0.3 fusion.14
  26.6 0.9 broadcast_multiply_fusion.1
  27.6 0.7 broadcast_compare_fusion
  28.3 1.6 pad_maximum_fusion.1.w_in_ref
  29.9 112.9 %shard_map.158 = (bf16[384,192,128]{2,1,0:T(8,128)(2,1)}, f32[16,73728]{1,0:T(8,128)}) custom-call(bf16[384,192,128]{2,1,0:T(8,128)(2,1)} %pair_ref.1, bf16[128,1024]{1,0:T(8,128)(2,1)} %pad_maximum_fusion.1.w_in_ref, bf16[512,128]{1,0:T(8,128)(2,1)} %w_down_ref.2, bf16[16,128]{1,0:T(8,128)(2,1)} %bitcast.43), custom_call_target="tpu_custom_call" | custom-call | tf_op jit(solution)/shard_map/pallas_call | solution.py:46
  142.8 6.2 reshape.62
  149.0 6.1 copy.22
  155.1 0.5 convolution_convert_fusion
  155.6 1.0 fusion.34
  156.9 3.7 fusion.35
  160.7 0.7 fusion.1
  161.4 2.3 fusion.2
  163.7 0.9 pad_maximum_fusion
  164.6 488.4 %shard_map.159 = (bf16[4,2,48,192,128]{4,3,2,1,0:T(8,128)(2,1)}, bf16[8,48,192,128]{3,2,1,0:T(8,128)(2,1)}, bf16[2,4,48,192,128]{4,3,2,1,0:T(8,128)(2,1)}) custom-call(bf16[2,4,48,192,128]{4,3,2,1,0:T(8,128)(2,1)} %bitcast.31), custom_call_target="tpu_custom_call" | custom-call | tf_op jit(solution)/shard_map/pallas_call | solution.py:210
  653.1 0.7 pad_maximum_fusion.2.w_in_ref
  653.8 86.2 %shard_map.160 = bf16[384,192,128]{2,1,0:T(8,128)(2,1)} custom-call(bf16[384,192,128]{2,1,0:T(8,128)(2,1)} %get-tuple-element.5.updated_ref, bf16[2,192,192,128]{3,2,1,0:T(8,128)(2,1)} %bitcast.35, bf16[128,1024]{1,0:T(8,128)(2,1)} %pad_maximum_fusion.2.w_in_ref, bf16[512,128]{1,0:T(8,128)(2,1)} %w_down_ref.3), custom_call_target="tpu_custom_call" | custom-call | tf_op jit(solution)/shard_map/pallas_call | solution.py:86
  740.0 3.5 copy.23
  743.7 1.7 fusion
  745.5 1.6 fusion.9
  (30 shorter events, 1.0 us)
Async XLA Ops:
  7.2 147.9 %copy-start = (bf16[384,384]{1,0:T(8,128)(2,1)S(1)}, bf16[384,384]{1,0:T(8,128)(2,1)}, u32[]{:S(2)}) copy-start(bf16[384,384]{1,0:T(8,128)(2,1)} %param.22) | copy-start | bytes 884740
  7.2 148.4 %all-reduce.2.cloned.1.call-start = ((), (), s32[]{:S(2)}) async-start(), calls=%async_computation | async-start | bytes 589824 | tf_op jit(solution)/shard_map/psum | solution.py:225
  26.2 713.8 %all-gather.3.cloned.1.call-start = ((), (), s32[]{:S(2)}) async-start(), calls=%async_computation.1 | async-start | bytes 5750784 | tf_op jit(solution)/shard_map/all_gather | solution.py:239
  164.6 488.4 %copy-start.2 = (bf16[128,512]{1,0:T(8,128)(2,1)S(1)}, bf16[128,512]{1,0:T(8,128)(2,1)}, u32[]{:S(2)}) copy-start(bf16[128,512]{1,0:T(8,128)(2,1)} %param.27) | copy-start | bytes 393220
  164.6 488.5 %copy-start.3 = (bf16[128,512]{1,0:T(8,128)(2,1)S(1)}, bf16[128,512]{1,0:T(8,128)(2,1)}, u32[]{:S(2)}) copy-start(bf16[128,512]{1,0:T(8,128)(2,1)} %param.28) | copy-start | bytes 393220
  743.5 1.9 copy-start.4
  743.5 1.9 copy-start.5
  743.7 3.4 copy-start.1
Sparse Core Ops, SparseCore 0:
  26.3 43.2 all-reduce.1
  164.7 72.1 all-gather.2
